TPU v7x, 512 devices: a whole 4x4x16 slice. The times are simulated.
512 devices in a mesh: ctx: 32 (over x_hi, z), head: 16 (over y, x_lo, core).
Axes of the slice: x: 4 (x_hi: 2, x_lo: 2; x = x_hi * 2 + x_lo), y: 4, z: 16, core: 2. Of those that a mesh axis runs over, the one named last changes fastest.
Arguments:
- queries: bfloat16 [4096, 12288], P('ctx', 'head'), may hold values from -400 to 400
- latents: bfloat16 [4096, 576], P('ctx'), may hold values from -1000 to 1000
- latent_gain: float32 [512], replicated, may hold values from 0.1 to 1.9
- latent_up: bfloat16 [512, 16384], P(None, 'head'), may hold values from -0.25 to 0.25
- out_weight: bfloat16 [8192, 7168], P('head', 'ctx'), may hold values from -0.75 to 0.75
- positions: int32 [4096], P('ctx'), may hold values from 0 to 4095, as said below
Outputs:
- mixed: bfloat16 [4096, 7168], P('ctx', 'head')
Inputs may be any that keep to these rules, and one draw needn't show every extreme that they name: The rows of one device hold two runs of 64 consecutive positions, each rising and starting at a multiple of 64; over the whole sequence every position appears once.
All inputs are finite; a program needn't handle non-finite values.
Results may differ from a plain program's by a relative error of at most 0.024.
Values may be sent and summed in bfloat16 or wider, within the bound.
A program may use at most 64 MiB of HBM per device.

v0:
```python
import math

import jax
import jax.numpy as jnp
from jax import lax
from jax.sharding import PartitionSpec as P

NOPE = 128
ROPE = 64
VDIM = 128
LATENT = 512


def rotate(values, angles):
    half_dim = values.shape[-1] // 2
    front_half = values[..., :half_dim]
    back_half = values[..., half_dim:]
    cosine = jnp.cos(angles)
    sine_part = jnp.sin(angles)
    return jnp.concatenate(
        [front_half * cosine - back_half * sine_part, back_half * cosine + front_half * sine_part],
        axis=-1,
    )


def angles_for(positions, width):
    half_dim = width // 2
    frequency = jnp.exp(
        jnp.arange(half_dim, dtype=jnp.float32) * (-2.0 * math.log(10000.0) / width)
    )
    return positions.astype(jnp.float32)[:, None] * frequency[None, :]


def compress(latents, latent_gain, positions):
    nope_part = latents[:, :LATENT].astype(jnp.float32)
    mean_square = jnp.mean(nope_part * nope_part, axis=-1, keepdims=True)
    normed = (nope_part * lax.rsqrt(mean_square + 1e-06) * latent_gain[None, :]).astype(
        jnp.bfloat16
    )
    angles = angles_for(positions, latents.shape[1] - LATENT)
    rotated = rotate(latents[:, LATENT:].astype(jnp.float32), angles).astype(jnp.bfloat16)
    return (normed, rotated, angles)


def shards(queries, latents, latent_gain, latent_up, out_weight, positions):
    normed, key_rope, angles = compress(latents, latent_gain, positions)
    packed = jnp.concatenate([normed, key_rope], axis=1)
    local_heads = latent_up.shape[1] // (NOPE + VDIM)
    tok_rows = queries.shape[0]
    grouped = queries.reshape(tok_rows, local_heads, NOPE + ROPE)
    query_nope = grouped[:, :, :NOPE]
    query_rope = rotate(grouped[:, :, NOPE:].astype(jnp.float32), angles[:, None, :]).astype(
        jnp.bfloat16
    )
    softmax_scale = (NOPE + ROPE) ** (-0.5)

    def update(running, block_rows, block_places):
        highest, totals, summed = running
        key_count = block_rows.shape[0]
        projected = jnp.dot(
            block_rows[:, :LATENT], latent_up, preferred_element_type=jnp.float32
        ).astype(jnp.bfloat16)
        projected = projected.reshape(key_count, local_heads, NOPE + VDIM)
        scores = jnp.einsum(
            "thd,nhd->htn", query_nope, projected[:, :, :NOPE], preferred_element_type=jnp.float32
        )
        scores = scores + jnp.einsum(
            "thr,nr->htn", query_rope, block_rows[:, LATENT:], preferred_element_type=jnp.float32
        )
        scores = scores * softmax_scale
        allowed = (block_places[None, :] <= positions[:, None])[None]
        raised = jnp.maximum(highest, jnp.max(jnp.where(allowed, scores, -1e30), axis=2))
        exp_scores = jnp.where(allowed, jnp.exp(scores - raised[:, :, None]), 0.0)
        rescale = jnp.exp(highest - raised)
        totals = totals * rescale + jnp.sum(exp_scores, axis=2)
        summed = summed * rescale[:, :, None] + jnp.einsum(
            "htn,nhv->htv",
            exp_scores.astype(jnp.bfloat16),
            projected[:, :, NOPE:],
            preferred_element_type=jnp.float32,
        )
        return (raised, totals, summed)

    def advance(running, block_in):
        block_rows, block_places = block_in
        running = update(running, block_rows, block_places)
        return (running, None)

    initial = (
        jnp.full((local_heads, tok_rows), -1e30, jnp.float32),
        jnp.zeros((local_heads, tok_rows), jnp.float32),
        jnp.zeros((local_heads, tok_rows, VDIM), jnp.float32),
    )
    running = initial
    rows_in = lax.all_gather(packed, "ctx", axis=0, tiled=True)
    pos_in = lax.all_gather(positions, "ctx", axis=0, tiled=True)
    key_count = rows_in.shape[0]
    sub_rows = 512
    blocks = key_count // sub_rows
    running, _ = lax.scan(
        advance,
        running,
        (rows_in.reshape(blocks, sub_rows, rows_in.shape[1]), pos_in.reshape(blocks, sub_rows)),
    )
    highest, totals, summed = running
    attended = (summed / totals[:, :, None]).astype(jnp.bfloat16)
    attended = jnp.transpose(attended, (1, 0, 2)).reshape(tok_rows, local_heads * VDIM)
    partial_out = jnp.dot(
        attended,
        lax.all_gather(out_weight, "ctx", axis=1, tiled=True),
        preferred_element_type=jnp.float32,
    )
    return lax.psum_scatter(
        partial_out.astype(jnp.bfloat16), "head", scatter_dimension=1, tiled=True
    )


def solution(mesh):
    in_specs = (P("ctx", "head"), P("ctx", None), P(), P(None, "head"), P("head", "ctx"), P("ctx"))
    out_specs = P("ctx", "head")
    return jax.shard_map(shards, mesh=mesh, in_specs=in_specs, out_specs=out_specs, check_vma=False)
```

profile of v0, /device:TPU:7, one launch (start us, length us, event | category | flops | bytes accessed | tf_op | source)
XLA Modules:
  0.0 442.2 jit_solution(13655509240275048136)
XLA Ops:
  7.3 1.0 fusion.13
  8.9 1.1 fusion.15
  11.6 1.1 copy.22
  12.9 66.3 %all-gather = s32[32,1,128]{2,1,0:T(1,128)S(1)} all-gather(s32[1,1,128]{2,1,0:T(1,128)} %bitcast.50), channel_id=1, replica_groups=mesh['ctx'=32,'head'=16] {'ctx'}, dimensions={0}, use_global_device_ids=true | all-gather | bytes 16896 | tf_op jit(solution)/shard_map/all_gather | solution.py:96
  80.6 96.0 %all-gather.4.cloned.1.call-done = bf16[4096,576]{0,1:T(8,128)(2,1)} async-done(((bf16[128,576]{0,1:T(8,128)(2,1)}), bf16[4096,576]{0,1:T(8,128)(2,1)}) %all-gather.4.cloned.1.call-update) | async-done | bytes 4718608 | tf_op jit(solution)/shard_map/all_gather | solution.py:95
  176.6 5.0 %copy.35 = bf16[72,8,8,512]{3,2,0,1:T(8,128)(2,1)} copy(bf16[72,8,8,512]{3,2,1,0:T(8,128)(2,1)} %bitcast.45) | data formatting | bytes 9437184 | tf_op jit(solution)/shard_map/reshape | solution.py:103
  181.6 52.3 %while.15 = (s32[]{:T(128)}, f32[4,128]{1,0:T(4,128)S(1)}, f32[4,128]{1,0:T(4,128)S(1)}, f32[4,128,128]{2,1,0:T(8,128)}, s32[8,512]{1,0:T(8,128)S(1)}, /*index=5...) while((s32[]{:T(128)}, f32[4,128]{1,0:T(4,128)S(1)}, ...), condition=%wide.region_4.5_spmd.clone, body=%wide.region_1.4_spmd.clone.sunk | while | flops 708053504 | bytes 17472192 | solution.py:100
  181.6 1.1 dynamic-slice_bitcast_fusion.2
  182.7 2.0 convolution_convert_fusion.3
  184.7 0.8 reshape.125
  188.1 1.1 dynamic-slice_bitcast_fusion.2
  189.2 2.0 convolution_convert_fusion.3
  191.2 0.8 reshape.125
  194.6 1.1 dynamic-slice_bitcast_fusion.2
  195.8 2.0 convolution_convert_fusion.3
  197.7 0.8 reshape.125
  201.2 1.1 dynamic-slice_bitcast_fusion.2
  202.3 2.0 convolution_convert_fusion.3
  204.3 0.8 reshape.125
  207.7 1.1 dynamic-slice_bitcast_fusion.2
  208.8 2.0 convolution_convert_fusion.3
  214.3 1.1 dynamic-slice_bitcast_fusion.2
  215.4 2.0 convolution_convert_fusion.3
  217.3 0.8 reshape.125
  220.8 1.1 dynamic-slice_bitcast_fusion.2
  221.9 2.0 convolution_convert_fusion.3
  227.3 1.1 dynamic-slice_bitcast_fusion.2
  228.4 2.0 convolution_convert_fusion.3
  233.9 1.1 copy.25
  235.0 126.2 %all-gather.6.cloned.1.call-done = bf16[512,7168]{0,1:T(8,128)(2,1)} async-done(((bf16[512,224]{0,1:T(8,128)(2,1)}), bf16[512,7168]{0,1:T(8,128)(2,1)}) %all-gather.6.cloned.1.call-update) | async-done | bytes 7340048 | tf_op jit(solution)/shard_map/all_gather | solution.py:110
  361.2 6.5 %convolution_convert_fusion.1 = bf16[128,7168]{0,1:T(8,128)(2,1)} fusion(bf16[512,7168]{0,1:T(8,128)(2,1)} %all-gather.6.cloned.1.call-done, bf16[128,512]{0,1:T(8,128)(2,1)S(1)} %bitcast.48), kind=kOutput, calls=%fused_computation.26 | convolution fusion | flops 940441600 | bytes 9306112 | tf_op jit(solution)/shard_map/dot_general | solution.py:108
  367.7 68.0 %reduce-scatter.2.cloned.1.call-done = bf16[128,448]{0,1:T(8,128)(2,1)} async-done(((bf16[128,7168]{0,1:T(8,128)(2,1)}), bf16[128,448]{0,1:T(8,128)(2,1)}) %reduce-scatter.2.cloned.1.call-update) | async-done | bytes 114704 | tf_op jit(solution)/shard_map/reduce_scatter | solution.py:113
  (141 shorter events, 27.5 us)
Async XLA Ops:
  6.5 170.1 %all-gather.4.cloned.1.call-start = ((), (), s32[]{:S(2)}) async-start(), calls=%async_computation.1 | async-start | bytes 4866048 | tf_op jit(solution)/shard_map/all_gather | solution.py:95
  10.8 350.4 %all-gather.6.cloned.1.call-start = ((), (), s32[]{:S(2)}) async-start(), calls=%async_computation.2 | async-start | bytes 7569408 | tf_op jit(solution)/shard_map/all_gather | solution.py:110
  11.6 424.1 %reduce-scatter.2.cloned.1.call-start = ((), (), s32[]{:S(2)}) async-start(), calls=%async_computation.3 | async-start | bytes 1949696 | tf_op jit(solution)/shard_map/reduce_scatter | solution.py:113
  176.6 5.0 %copy-start.2 = (s32[128]{0:T(128)S(1)}, s32[128]{0:T(128)}, u32[]{:S(2)}) copy-start(s32[128]{0:T(128)} %param.13) | copy-start | bytes 1540
  185.5 1.4 copy-start
  187.4 0.7 copy-start.1
  192.0 1.4 copy-start
  193.9 0.7 copy-start.1
  198.5 1.4 copy-start
  200.5 0.7 copy-start.1
  205.1 1.4 copy-start
  207.0 0.7 copy-start.1
  211.6 1.4 copy-start
  213.6 0.7 copy-start.1
  218.1 1.4 copy-start
  220.1 0.7 copy-start.1
  224.7 1.4 copy-start
  226.6 0.7 copy-start.1
  231.2 1.4 copy-start
  233.2 0.7 copy-start.1
Sparse Core Ops, SparseCore 0:
  10.9 165.6 all-gather.3
  179.7 181.4 all-gather.5
  367.8 67.8 reduce-scatter.1
where the time goes:
time: 451 us; the launch traced here: 442 us
  waiting for transfers between devices  291 us (65%)
  blocking collectives  66.3 us (15%)
  local copies, waits for them, and re-layouts  31.5 us (7%)
  matrix products  31.3 us (7%)
  between operations  13.2 us (3%)
  other arithmetic  7.97 us (2%)
    all_gather x1, waiting for transfers between devices, shards(): lax.all_gather(out_weight, 'ctx', axis=1, tiled=True)  126 us
    all_gather x1, waiting for transfers between devices, shards(): rows_in = lax.all_gather(packed, 'ctx', axis=0, tiled=True)  96 us
    reduce_scatter x1, waiting for transfers between devices, shards(): lax.psum_scatter(partial_out.astype(jnp.bfloat16), 'head', scatter_dimens...  68 us
    all_gather x1, blocking collectives, shards(): pos_in = lax.all_gather(positions, 'ctx', axis=0, tiled=True)  66.3 us
    dot_general x8, matrix products, update(): jnp.dot(block_rows[:, :LATENT], latent_up, preferred_element_type=jnp.flo...  15.6 us
  transfers between devices with their start and end apart: 3, of which 3 were waited for; matrix products, arithmetic and copies ran while one was open for 12% of the time, Pallas kernels for 0%

commit v1 on v0

v1 whole, which is shorter than its diff:
```python
import math

import jax
import jax.numpy as jnp
from jax import lax
from jax.experimental import pallas as pl
from jax.experimental.pallas import tpu as pltpu
from jax.sharding import PartitionSpec as P

NOPE = 128
ROPE = 64
VDIM = 128
LATENT = 512
WIDE = LATENT + 128
HEADS = 4
MASKED = -1e30
MESH = pl.DeviceIdType.MESH
F32 = jnp.float32
BF16 = jnp.bfloat16


def dot_nt(a, b):
    return lax.dot_general(a, b, (((1,), (1,)), ((), ())), preferred_element_type=F32)


def kernel(
    q_ref, lat_ref, gain_ref, up_ref, wo_ref, pos_ref, out_ref,
    own, kb, qb, wb, ab, acc, high, total, posq, bias,
    o_out, o_in, lse_out, lse_in, stage, parts,
    za_s, za_r, zb_s, zb_r, k1_s, k2_s, k_r, wx_s, wx_r, q_s, q_r,
    w_s, w_r, m_s, m_r, a_s, a_r, p_s, p_r,
):
    c = lax.axis_index("ctx")
    h = lax.axis_index("head")
    xh, z = c // 16, c % 16
    y, xl, core = h // 4, (h // 2) % 2, h % 2
    x = xh * 2 + xl
    chip = h // 2
    other = 1 - core

    def dev(x_, y_, z_, core_):
        return ((x_ // 2) * 16 + z_, y_ * 4 + (x_ % 2) * 2 + core_)

    def remote(src, dst, send, recv, to):
        return pltpu.make_async_remote_copy(
            src_ref=src, dst_ref=dst, send_sem=send, recv_sem=recv, device_id=to, device_id_type=MESH
        )

    barrier = pltpu.get_barrier_semaphore()
    z_offsets = (1, 15, 2, 14, 4, 12, 8)
    for o in z_offsets:
        pl.semaphore_signal(barrier, inc=1, device_id=dev(x, y, (z + o) % 16, core), device_id_type=MESH)
    for dx in range(4):
        for dy in range(4):
            for dk in range(2):
                if dx or dy or dk:
                    to = dev((x + dx) % 4, (y + dy) % 4, z, (core + dk) % 2)
                    pl.semaphore_signal(barrier, inc=1, device_id=to, device_id_type=MESH)

    pos = pos_ref[...]
    posf = pos.astype(F32)
    freq = jnp.exp(
        lax.broadcasted_iota(jnp.int32, (ROPE // 2, 128), 0).astype(F32) * (-2.0 * math.log(10000.0) / ROPE)
    )
    angles = posf * freq
    cosine, sine = jnp.cos(angles), jnp.sin(angles)
    nope = lat_ref[:LATENT, :].astype(F32)
    mean_square = jnp.mean(nope * nope, axis=0, keepdims=True)
    nope = nope * lax.rsqrt(mean_square + 1e-06)
    front = lat_ref[LATENT : LATENT + 32, :].astype(F32)
    back = lat_ref[LATENT + 32 :, :].astype(F32)
    row = lax.broadcasted_iota(jnp.int32, (64, 128), 0)
    places = jnp.where(
        row == 0, jnp.right_shift(pos, 6).astype(F32), jnp.where(row == 1, jnp.bitwise_and(pos, 63).astype(F32), 0.0)
    )
    tail = jnp.concatenate([front * cosine - back * sine, back * cosine + front * sine, places], axis=0)
    own[:, :LATENT] = (nope.T * gain_ref[...]).astype(BF16)
    own[:, LATENT:] = tail.T.astype(BF16)
    posq[...] = jnp.broadcast_to(posf, (128, 128)).T
    wb[z, core] = wo_ref[pl.ds(pl.multiple_of(core * 112, 16), 112), :]

    pl.semaphore_wait(barrier, 38)

    mine = (z % 2) == core
    slice_rows = pl.ds(pl.multiple_of(chip * 16, 16), 16)

    def za_copy(a):
        return remote(
            own.at[slice_rows], kb.at[0, y, x, pl.ds(16 * a, 16)], za_s.at[a - 1], za_r.at[a - 1],
            dev(x, y, (z + 4 * a) % 16, core),
        )

    @pl.when(mine)
    def _():
        for a in (1, 3, 2):
            za_copy(a).start()
        kb[0, y, x, 0:16, :] = own[slice_rows, :]

    wx = remote(
        wo_ref.at[pl.ds(pl.multiple_of(other * 112, 16), 112)], wb.at[z, core], wx_s, wx_r, dev(x, y, z, other)
    )
    wx.start()

    def unit_place(way, u):
        dist = u // 2 + 1
        head = core if u % 2 == 0 and not (u == 14 and way == 1) else other
        held = (z - (dist - 1)) % 16 if way == 0 else (z + (dist - 1)) % 16
        near = (z + 1) % 16 if way == 0 else (z + 15) % 16
        return held, near, head

    def w_copy(way, u):
        held, near, head = unit_place(way, u)
        return remote(
            wb.at[held, head], wb.at[held, head], w_s.at[way, u], w_r.at[way, u], dev(x, y, near, core)
        )

    def w_wait(way, u):
        dist = u // 2 + 1
        block = (z - dist) % 16 if way == 0 else (z + dist) % 16
        head = unit_place(way, u)[2]
        remote(
            wb.at[block, head], wb.at[block, head], w_s.at[way, u], w_r.at[way, u], dev(x, y, z, other)
        ).wait_recv()

    def serve(u):
        for way in (0, 1):
            w_wait(way, u)
            if u < 12:
                w_copy(way, u + 2).start()
            elif (u, way) in ((12, 0), (13, 1)):
                w_copy(way, 14).start()

    for way in (0, 1):
        w_copy(way, 0).start()

    scale = (NOPE + ROPE) ** -0.5 * math.log2(math.e)
    cos_all = jnp.concatenate([cosine] * 4, axis=0).T
    sin_all = jnp.concatenate([-sine, sine, -sine, sine], axis=0).T
    lane = lax.broadcasted_iota(jnp.int32, (128, 128), 1)
    for pair in range(HEADS // 2):
        both = q_ref[:, pair * 384 : (pair + 1) * 384]
        rest = pltpu.roll(both[:, 128:].astype(F32), 192, 1)
        ropes = rest[:, 128:]
        swapped = jnp.where((lane // 32) % 2 == 0, pltpu.roll(ropes, 96, 1), pltpu.roll(ropes, 32, 1))
        turned = (ropes * cos_all + swapped * sin_all) * scale
        for i in range(2):
            n = pair * 2 + i
            plain = both[:, :128] if i == 0 else rest[:, :128].astype(BF16)
            absorbed = dot_nt(plain, up_ref[:, 256 * n : 256 * n + 128]) * scale
            rope = pltpu.roll(turned, 64, 1) if i == 0 else turned
            qb[core * 4 + n, :, :LATENT] = absorbed.astype(BF16)
            qb[core * 4 + n, :, LATENT:] = jnp.where(lane < 64, rope, 0.0).astype(BF16)
    q_copy = remote(
        qb.at[pl.ds(core * 4, 4)], qb.at[pl.ds(core * 4, 4)], q_s, q_r, dev(x, y, z, other)
    )
    q_copy.start()

    wx_in = remote(wb.at[z, other], wb.at[z, other], wx_s, wx_r, dev(x, y, z, other))
    wx_in.wait_recv()
    for way in (0, 1):
        w_copy(way, 1).start()

    def zb_copy(i):
        dst = kb.at[0, y, x] if i == 0 else kb.at[1, x, y]
        to = (z + (1, 15, 2)[i]) % 16
        return remote(kb.at[0, y, x], dst, zb_s.at[i], zb_r.at[min(i, 1)], dev(x, y, to, core))

    def zb_wait(half):
        dst = kb.at[0, y, x] if half == 0 else kb.at[1, x, y]
        remote(dst, dst, zb_s.at[0], zb_r.at[half], dev(x, y, z, other)).wait_recv()

    @pl.when(mine)
    def _():
        for a in (1, 3, 2):
            za_copy(a).wait_recv()
        for i in range(3):
            zb_copy(i).start()

    @pl.when(jnp.logical_not(mine))
    def _():
        zb_wait(0)

    def place(f):
        return (y, x) if f == 0 else (x, y)

    def peer(f, along_a, i):
        moves_y = (f == 0) == along_a
        if moves_y:
            return dev(x, (y + i) % 4, z, core)
        return dev((x + i) % 4, y, z, core)

    def k1_copy(f, along_a, i):
        a, b = place(f)
        return remote(
            kb.at[f, a, b], kb.at[f, a, b], k1_s.at[f, int(along_a) * 3 + i - 1], k_r.at[f, a, b], peer(f, along_a, i)
        )

    def k2_copy(f, j, i):
        a, b = place(f)
        b = (b + j) % 4
        return remote(
            kb.at[f, a, b], kb.at[f, a, b], k2_s.at[f, j - 1, i - 1], k_r.at[f, a, b], peer(f, True, i)
        )

    def k_wait(f, a, b):
        remote(
            kb.at[f, a, b], kb.at[f, a, b], k1_s.at[f, 0], k_r.at[f, a, b], dev(x, y, z, other)
        ).wait_recv()

    for i in (1, 3, 2):
        k1_copy(0, False, i).start()
    for i in (1, 3, 2):
        k1_copy(0, True, i).start()
    zb_wait(1)
    for i in (1, 3, 2):
        k1_copy(1, False, i).start()
    for i in (1, 3, 2):
        k1_copy(1, True, i).start()

    serve(0)
    for j in (1, 3, 2):
        for f in (0, 1):
            a, b = place(f)
            k_wait(f, a, (b + j) % 4)
            for i in (1, 3, 2):
                k2_copy(f, j, i).start()
    serve(1)

    high[...] = jnp.full_like(high, MASKED)
    total[...] = jnp.zeros_like(total)
    acc[...] = jnp.zeros_like(acc)
    remote(
        qb.at[pl.ds(other * 4, 4)], qb.at[pl.ds(other * 4, 4)], q_s, q_r, dev(x, y, z, other)
    ).wait_recv()
    lane8 = lax.broadcasted_iota(jnp.int32, (8, WIDE), 1)
    pick = jnp.where(
        lane8 == LATENT + ROPE, 64.0, jnp.where(lane8 == LATENT + ROPE + 1, 1.0, 0.0)
    ).astype(BF16)

    def attend(f, a):
        keys = kb[f, a].reshape(256, WIDE)
        posk = dot_nt(pick, keys)[0:1, :]
        for i in range(2):
            bias[:, i * 128 : (i + 1) * 128] = jnp.where(posk[:, i * 128 : (i + 1) * 128] <= posq[...], 0.0, MASKED)

        def rows(p, carry):
            queries = qb[pl.ds(p * 2, 2)].reshape(256, WIDE)
            block = kb[f, a].reshape(256, WIDE)
            masks = bias[...]
            scores = dot_nt(queries, block) + jnp.concatenate([masks, masks], axis=0)
            before = high[p]
            raised = jnp.maximum(before, jnp.max(scores, axis=1, keepdims=True))
            terms = jnp.exp2(scores - raised[:, :1])
            rescale = jnp.exp2(before - raised)
            high[p] = raised
            total[p] = total[p] * rescale + terms[:, :128] + terms[:, 128:]
            acc[p] = acc[p] * rescale[:, :1] + jnp.dot(
                terms.astype(BF16), block[:, :LATENT], preferred_element_type=F32
            )
            return carry

        lax.fori_loop(0, 4, rows, 0)

    step = 2
    for i in (0, 1, 3, 2):
        for f in (0, 1):
            a, b = place(f)
            a = (a + i) % 4
            if i:
                for j in range(4):
                    k_wait(f, a, (b + j) % 4)
            attend(f, a)
            serve(step)
            step += 1

    for t in range(2):
        p = other * 2 + t
        sums = jnp.sum(total[p], axis=1, keepdims=True)
        o_out[t] = (acc[p] / sums).astype(BF16)
        lse_out[t] = high[p] + jnp.log2(sums)
    m_copies = [
        remote(o_out, o_in, m_s.at[0], m_r.at[0], dev(x, y, z, other)),
        remote(lse_out, lse_in, m_s.at[1], m_r.at[1], dev(x, y, z, other)),
    ]
    for copy in m_copies:
        copy.start()
    serve(step)
    for copy in m_copies:
        copy.wait_recv()
    for t in range(2):
        p = core * 2 + t
        sums = jnp.sum(total[p], axis=1, keepdims=True)
        lse = high[p] + jnp.log2(sums)
        largest = jnp.maximum(lse, lse_in[t])
        one, two = jnp.exp2(lse - largest), jnp.exp2(lse_in[t] - largest)
        share = two / (one + two)
        merged = acc[p] * ((one / (one + two))[:, :1] / sums) + o_in[t].astype(F32) * share[:, :1]
        merged = merged.astype(BF16)
        for i in range(2):
            n = t * 2 + i
            ab[core, xh, :, n * 128 : (n + 1) * 128] = jnp.dot(
                merged[i * 128 : (i + 1) * 128], up_ref[:, 256 * n + 128 : 256 * n + 256], preferred_element_type=F32
            ).astype(BF16)

    x2 = (x + 2) % 4
    a_copies = [
        remote(ab.at[core, xh], ab.at[core, xh], a_s.at[i], a_r.at[core, xh], to)
        for i, to in enumerate((dev(x2, y, z, core), dev(x2, y, z, other), dev(x, y, z, other)))
    ]
    for copy in a_copies:
        copy.start()
    serve(step + 1)
    for k, r in ((other, xh), (core, 1 - xh), (other, 1 - xh)):
        remote(ab.at[k, r], ab.at[k, r], a_s.at[0], a_r.at[k, r], dev(x, y, z, other)).wait_recv()

    def p_copy(zb, r):
        head = (xh * 16 + zb) // 2
        dst = parts.at[chip, zb % 2, core]
        return (
            jnp.logical_and(head == h, xh == r),
            remote(stage.at[zb, r], dst, p_s.at[zb, r], p_r, (r * 16 + z, head)),
            pltpu.make_async_copy(stage.at[zb, r], dst, p_r),
        )

    def project(zb):
        made = dot_nt(wb[zb, 0], ab[0].reshape(256, 512)) + dot_nt(wb[zb, 1], ab[1].reshape(256, 512))
        made = made.astype(BF16)
        for r in range(2):
            stage[zb, r] = made[:, r * 128 : (r + 1) * 128]
            stays, far, near = p_copy(zb, r)
            pl.when(jnp.logical_not(stays))(far.start)
            pl.when(stays)(near.start)

    def project_both(dist):
        def one(i, carry):
            project((z + jnp.where(i == 0, dist, 16 - dist)) % 16)
            return carry

        lax.fori_loop(0, 2, one, 0)

    project(z)
    for dist in range(1, 5):
        project_both(dist)
    serve(12)
    project_both(5)
    project_both(6)
    serve(13)
    project_both(7)
    serve(14)
    project((z + 8) % 16)

    remote(parts, parts, p_s.at[0, 0], p_r, dev(x, y, z, other)).wait_recv()
    result = parts[0].reshape(448, 128).astype(F32)
    for i in range(1, 8):
        result = result + parts[i].reshape(448, 128).astype(F32)
    out_ref[...] = result.astype(BF16)

    @pl.when(mine)
    def _():
        for a in (1, 3, 2):
            za_copy(a).wait_send()
        for i in range(3):
            zb_copy(i).wait_send()

    for f in (0, 1):
        for i in (1, 2, 3):
            k1_copy(f, False, i).wait_send()
            k1_copy(f, True, i).wait_send()
            for j in (1, 2, 3):
                k2_copy(f, j, i).wait_send()
    wx.wait_send()
    q_copy.wait_send()
    for way in (0, 1):
        for u in range(15):
            w_copy(way, u).wait_send()
    for copy in m_copies + a_copies:
        copy.wait_send()

    def p_done(zb, carry):
        for r in range(2):
            stays, far, _ = p_copy(zb, r)
            pl.when(jnp.logical_not(stays))(far.wait_send)
        return carry

    lax.fori_loop(0, 16, p_done, 0)


def shards(queries, latents, latent_gain, latent_up, out_weight, positions):
    dma = pltpu.SemaphoreType.DMA
    vmem = pltpu.VMEM
    made = pl.pallas_call(
        kernel,
        out_shape=jax.ShapeDtypeStruct((448, 128), BF16),
        in_specs=[pl.BlockSpec(memory_space=pltpu.VMEM)] * 6,
        out_specs=pl.BlockSpec(memory_space=pltpu.VMEM),
        scratch_shapes=[
            vmem((128, WIDE), BF16),
            vmem((2, 4, 4, 64, WIDE), BF16),
            vmem((8, 128, WIDE), BF16),
            vmem((16, 2, 112, 512), BF16),
            vmem((2, 2, 128, 512), BF16),
            vmem((4, 256, 512), F32),
            vmem((4, 256, 128), F32),
            vmem((4, 256, 128), F32),
            vmem((128, 128), F32),
            vmem((128, 256), F32),
            vmem((2, 256, 512), BF16),
            vmem((2, 256, 512), BF16),
            vmem((2, 256, 128), F32),
            vmem((2, 256, 128), F32),
            vmem((16, 2, 112, 128), BF16),
            vmem((8, 2, 2, 112, 128), BF16),
            dma((3,)), dma((3,)), dma((3,)), dma((2,)),
            dma((2, 6)), dma((2, 3, 3)), dma((2, 4, 4)),
            dma, dma, dma, dma,
            dma((2, 15)), dma((2, 15)), dma((2,)), dma((2,)),
            dma((3,)), dma((2, 2)), dma((16, 2)), dma,
        ],
        compiler_params=pltpu.CompilerParams(
            collective_id=0, has_side_effects=True, vmem_limit_bytes=48 * 1024 * 1024
        ),
        cost_estimate=pl.CostEstimate(flops=8_000_000_000, bytes_accessed=4_000_000, transcendentals=2_200_000),
    )(
        queries, latents.T, latent_gain.reshape(1, 512), latent_up, out_weight.T, positions.reshape(1, 128)
    )
    return made.T


def solution(mesh):
    in_specs = (P("ctx", "head"), P("ctx", None), P(), P(None, "head"), P("head", "ctx"), P("ctx"))
    out_specs = P("ctx", "head")
    return jax.shard_map(shards, mesh=mesh, in_specs=in_specs, out_specs=out_specs, check_vma=False)
```

time: 451 us -> 102 us (0.23); the launches traced: 442 us -> 101 us
  waiting for transfers between devices: 291 us -> 0 us
  Pallas kernels: 0 us -> 95.3 us
  blocking collectives: 66.3 us -> 0 us
  matrix products: 31.3 us -> 0 us
  local copies, waits for them, and re-layouts: 31.5 us -> 5.33 us
  between operations: 13.2 us -> 0.02 us
  other arithmetic: 7.97 us -> 0 us
    all_gather x2 -> x0, waiting for transfers between devices: 222 us -> none  [the longest x1 126 us: shards(): lax.all_gather(out_weight, 'ctx', axis=1, tiled=True)]
    pallas_call x0 -> x1, Pallas kernels: none -> 95.3 us  [shards(): pl.pallas_call(kernel, out_shape=jax.ShapeDtypeStruct((448, 128), BF16),...]
    reduce_scatter x1 -> x0, waiting for transfers between devices: 68 us -> none  [shards(): lax.psum_scatter(partial_out.astype(jnp.bfloat16), 'head', scatter_dimens...]
    all_gather x1 -> x0, blocking collectives: 66.3 us -> none  [shards(): pos_in = lax.all_gather(positions, 'ctx', axis=0, tiled=True)]
    dot_general x33 -> x0, matrix products: 31.3 us -> none  [the longest x8 15.6 us: update(): jnp.dot(block_rows[:, :LATENT], latent_up, preferred_element_type=jnp.flo...]
    reshape x10 -> x0, local copies, waits for them, and re-layouts: 11.4 us -> none  [the longest x8 6.37 us: update(): projected = projected.reshape(key_count, local_heads, NOPE + VDIM)]
    squeeze x8 -> x0, local copies, waits for them, and re-layouts: 8.86 us -> none  [shards(): lax.scan(advance, running, (rows_in.reshape(blocks, sub_rows, rows_in.sha...]
    while x41 -> x0, local copies, waits for them, and re-layouts: 6.52 us -> none
  transfers between devices with their start and end apart: 3 -> 0, of which waited for: 3 -> 0; matrix products, arithmetic and copies ran while one was open for 12% -> 0% of each run, Pallas kernels for 0% -> 0%
where the time goes in v1:
time: 102 us; the launch traced here: 101 us
  Pallas kernels  95.3 us (93%)
  local copies, waits for them, and re-layouts  5.33 us (5%)
    pallas_call x1, Pallas kernels, shards(): pl.pallas_call(kernel, out_shape=jax.ShapeDtypeStruct((448, 128), BF16),...  95.3 us
    unnamed x13, local copies, waits for them, and re-layouts  5.33 us

profile of v1, /device:TPU:7, one launch (start us, length us, event | category | flops | bytes accessed | tf_op | source)
XLA Modules:
  0.0 100.7 jit_solution(15287535277786738407)
XLA Ops:
  0.0 0.0 copy-start.4
  0.0 0.0 copy-start.5
  0.0 0.7 copy-done.4
  0.7 0.0 copy-done.5
  0.7 0.0 copy-start
  0.7 1.2 %copy-done = bf16[512,1024]{1,0:T(8,128)(2,1)S(1)} copy-done((bf16[512,1024]{1,0:T(8,128)(2,1)S(1)}, bf16[512,1024]{1,0:T(8,128)(2,1)}, u32[]{:S(2)}) %copy-start) | copy-done | bytes 1048600
  1.9 0.0 copy-start.1
  1.9 0.9 copy-done.1
  2.9 0.0 copy-start.2
  2.9 0.9 copy-done.2
  3.8 0.0 copy-start.3
  3.8 0.9 copy-done.3
  4.7 95.3 %shard_map.64 = bf16[448,128]{1,0:T(8,128)(2,1)S(1)} custom-call(bf16[128,768]{1,0:T(8,128)(2,1)S(1)} %copy-done.2, bf16[576,128]{1,0:T(8,128)(2,1)S(1)} %bitcast.7, f32[1,512]{1,0:T(1,128)S(1)} %bitcast.8, bf16[512,1024]{1,0:T(8,128)(2,1)S(1)} %copy-done, bf16[224,512]{1,0:T(8,128)(2,1)S(1)} %bitcast.6, s32[1,128]{1,0:T(1,128)S(1)} %bitcast.9), custom_call_target="tpu_custom_call" | custom-call | flops 8000000000 | bytes 4000000 | tf_op jit(solution)/shard_map/pallas_call | solution.py:391
  100.0 0.6 copy.8
Async XLA Ops:
  0.0 0.7 copy-start.4
  0.0 0.7 copy-start.5
  0.7 1.2 %copy-start = (bf16[512,1024]{1,0:T(8,128)(2,1)S(1)}, bf16[512,1024]{1,0:T(8,128)(2,1)}, u32[]{:S(2)}) copy-start(bf16[512,1024]{1,0:T(8,128)(2,1)} %up_ref.1) | copy-start | bytes 3145732
  1.9 0.9 copy-start.1
  2.9 0.9 copy-start.2
  3.8 0.9 copy-start.3

commit v2 on v1

v2 whole, which is shorter than its diff:
```python
import functools
import math

import jax
import jax.numpy as jnp
from jax import lax
from jax.experimental import pallas as pl
from jax.experimental.pallas import tpu as pltpu
from jax.sharding import PartitionSpec as P

NOPE = 128
ROPE = 64
VDIM = 128
LATENT = 512
WIDE = LATENT + 128
HEADS = 4
MASKED = -1e30
MESH = pl.DeviceIdType.MESH
F32 = jnp.float32
BF16 = jnp.bfloat16


def dot_nt(a, b):
    return lax.dot_general(a, b, (((1,), (1,)), ((), ())), preferred_element_type=F32)


def kernel(
    q_hbm, lat_hbm, gain_hbm, up_hbm, wo_hbm, pos_hbm, out_ref,
    q_ref, lat_ref, gain_ref, up_ref, pos_ref,
    own, kb, qb, wb, ab, scores, posq, bias,
    o_out, o_in, lse_out, lse_in, stage, parts,
    z_s, z_r, k1_s, k2_s, k3_s, k_r, wx_s, wx_r, q_s, q_r,
    w_s, w_r, m_s, m_r, a_s, a_r, p_s, p_r, in_s,
):
    c = lax.axis_index("ctx")
    h = lax.axis_index("head")
    xh, z = c // 16, c % 16
    y, xl, core = h // 4, (h // 2) % 2, h % 2
    x = xh * 2 + xl
    chip = h // 2
    other = 1 - core

    def dev(x_, y_, z_, core_):
        return ((x_ // 2) * 16 + z_, y_ * 4 + (x_ % 2) * 2 + core_)

    def remote(src, dst, send, recv, to):
        return pltpu.make_async_remote_copy(
            src_ref=src, dst_ref=dst, send_sem=send, recv_sem=recv, device_id=to, device_id_type=MESH
        )

    loads = [
        pltpu.make_async_copy(src, dst, in_s.at[i])
        for i, (src, dst) in enumerate((
            (pos_hbm, pos_ref), (lat_hbm, lat_ref), (gain_hbm, gain_ref), (q_hbm, q_ref), (up_hbm, up_ref),
            (wo_hbm.at[pl.ds(pl.multiple_of(core * 112, 16), 112)], wb.at[core, 0]),
        ))
    ]
    for load in loads:
        load.start()

    barrier = pltpu.get_barrier_semaphore()
    for o in range(1, 16):
        pl.semaphore_signal(barrier, inc=1, device_id=dev(x, y, (z + o) % 16, core), device_id_type=MESH)
    for dx in range(4):
        for dy in range(4):
            for dk in range(2):
                if dx or dy or dk:
                    to = dev((x + dx) % 4, (y + dy) % 4, z, (core + dk) % 2)
                    pl.semaphore_signal(barrier, inc=1, device_id=to, device_id_type=MESH)


    wx = remote(
        wo_hbm.at[pl.ds(pl.multiple_of(other * 112, 16), 112)], wb.at[core, 0], wx_s, wx_r, dev(x, y, z, other)
    )
    pl.semaphore_wait(barrier, 46)
    wx.start()

    def slot_of(way, dist):
        return 0 if dist == 0 else 15 if dist == 8 else 2 * dist - 1 + way

    def w_copy(way, u):
        dist = u // 2 + 1
        head = core if u % 2 == 0 and not (u == 14 and way == 1) else other
        near = (z + 1) % 16 if way == 0 else (z + 15) % 16
        return remote(
            wb.at[head, slot_of(way, dist - 1)], wb.at[head, slot_of(way, dist)],
            w_s.at[way, u], w_r.at[way, u], dev(x, y, near, core),
        )

    def w_wait(way, u):
        w_copy(way, u).wait_recv()

    def serve(u):
        for way in (0, 1):
            w_wait(way, u)
            if u < 12:
                w_copy(way, u + 2).start()
            elif (u, way) in ((12, 0), (13, 1)):
                w_copy(way, 14).start()

    loads[5].wait()
    for way in (0, 1):
        w_copy(way, 0).start()

    for load in loads[:3]:
        load.wait()

    pos = pos_ref[...]
    posf = pos.astype(F32)
    freq = jnp.exp(
        lax.broadcasted_iota(jnp.int32, (ROPE // 2, 128), 0).astype(F32) * (-2.0 * math.log(10000.0) / ROPE)
    )
    angles = posf * freq
    cosine, sine = jnp.cos(angles), jnp.sin(angles)
    nope = lat_ref[:LATENT, :].astype(F32)
    mean_square = jnp.mean(nope * nope, axis=0, keepdims=True)
    nope = nope * lax.rsqrt(mean_square + 1e-06)
    front = lat_ref[LATENT : LATENT + 32, :].astype(F32)
    back = lat_ref[LATENT + 32 :, :].astype(F32)
    row = lax.broadcasted_iota(jnp.int32, (64, 128), 0)
    places = jnp.where(
        row == 0, jnp.right_shift(pos, 6).astype(F32), jnp.where(row == 1, jnp.bitwise_and(pos, 63).astype(F32), 0.0)
    )
    tail = jnp.concatenate([front * cosine - back * sine, back * cosine + front * sine, places], axis=0)
    own[:, :LATENT] = (nope.T * gain_ref[...]).astype(BF16)
    own[:, LATENT:] = tail.T.astype(BF16)
    posq[...] = jnp.broadcast_to(posf, (128, 128)).T

    mine = (z % 2) == core
    slice_rows = pl.ds(pl.multiple_of(chip * 16, 16), 16)
    from_even = (0, -2, 2, -4, 4, -6, 6, 8)
    from_odd = (-1, 1, -3, 3, -5, 5, -7, 7)

    def place(f):
        return (y, x) if f == 0 else (x, y)

    def slice_at(n):
        f, t = (n // 2) % 2, n // 4
        return kb.at[(f, *place(f), pl.ds(32 * t + 16 * (n % 2), 16))]

    def z_copy(o):
        n = from_odd.index(-o) if o % 2 else from_even.index(8 if o == 8 else -o)
        return remote(
            own.at[slice_rows], slice_at(n), z_s.at[o % 16 - 1], z_r.at[n], dev(x, y, (z + o) % 16, core)
        )

    def z_wait(n):
        remote(slice_at(n), slice_at(n), z_s.at[0], z_r.at[n], dev(x, y, z, other)).wait_recv()

    z_order = (1, -1, 2, -2, 3, -3, 4, -4, 5, -5, 6, -6, 7, -7, 8)

    @pl.when(mine)
    def _():
        for o in z_order:
            z_copy(o).start()
        kb[0, y, x, 0:16, :] = own[slice_rows, :]

    wx_in = remote(wb.at[other, 0], wb.at[other, 0], wx_s, wx_r, dev(x, y, z, other))
    wx_in.wait_recv()
    for way in (0, 1):
        w_copy(way, 1).start()

    for load in loads[3:5]:
        load.wait()
    scale = (NOPE + ROPE) ** -0.5 * math.log2(math.e)
    cos_all = jnp.concatenate([cosine] * 4, axis=0).T
    sin_all = jnp.concatenate([-sine, sine, -sine, sine], axis=0).T
    lane = lax.broadcasted_iota(jnp.int32, (128, 128), 1)
    for pair in range(HEADS // 2):
        both = q_ref[:, pair * 384 : (pair + 1) * 384]
        rest = pltpu.roll(both[:, 128:].astype(F32), 192, 1)
        ropes = rest[:, 128:]
        swapped = jnp.where((lane // 32) % 2 == 0, pltpu.roll(ropes, 96, 1), pltpu.roll(ropes, 32, 1))
        turned = (ropes * cos_all + swapped * sin_all) * scale
        for i in range(2):
            n = pair * 2 + i
            plain = both[:, :128] if i == 0 else rest[:, :128].astype(BF16)
            absorbed = dot_nt(plain, up_ref[:, 256 * n : 256 * n + 128]) * scale
            rope = pltpu.roll(turned, 64, 1) if i == 0 else turned
            qb[core * 4 + n, :, :LATENT] = absorbed.astype(BF16)
            qb[core * 4 + n, :, LATENT:] = jnp.where(lane < 64, rope, 0.0).astype(BF16)
    q_copy = remote(
        qb.at[pl.ds(core * 4, 4)], qb.at[pl.ds(core * 4, 4)], q_s, q_r, dev(x, y, z, other)
    )
    q_copy.start()

    def peer(f, along_a, i):
        moves_y = (f == 0) == along_a
        if moves_y:
            return dev(x, (y + i) % 4, z, core)
        return dev((x + i) % 4, y, z, core)

    def piece(f, a, b, t):
        return kb.at[f, a, b, pl.ds(32 * t, 32)], k_r.at[f, a, b, t]

    def k1_copy(f, t, i):
        a, b = place(f)
        ref, got = piece(f, a, b, t)
        return remote(ref, ref, k1_s.at[f, t, i - 1], got, peer(f, False, i))

    def k2_copy(f, t, j, side):
        a, b = place(f)
        ref, got = piece(f, a, (b + j) % 4, t)
        return remote(ref, ref, k2_s.at[f, t, j, side], got, peer(f, True, 1 if side == 0 else 3))

    def k3_copy(f, t, j):
        a, b = place(f)
        ref, got = piece(f, (a + (3, 1)[t]) % 4, (b + j) % 4, t)
        return remote(ref, ref, k3_s.at[f, t, j], got, peer(f, True, (1, 3)[t]))

    def k_wait(f, t, i, j):
        a, b = place(f)
        ref, got = piece(f, (a + i) % 4, (b + j) % 4, t)
        remote(ref, ref, k3_s.at[f, t, 0], got, dev(x, y, z, other)).wait_recv()

    for part in range(4):
        f, t = part % 2, part // 2
        if part == 0:
            pl.when(jnp.logical_not(mine))(functools.partial(z_wait, 0))
        else:
            z_wait(2 * part)
        z_wait(2 * part + 1)
        for i in (1, 3, 2):
            k1_copy(f, t, i).start()
        for side in (0, 1):
            k2_copy(f, t, 0, side).start()
        serve(part)

    def spread(t):
        for j in (1, 3, 2):
            for f in (0, 1):
                k_wait(f, t, 0, j)
                for side in (0, 1):
                    k2_copy(f, t, j, side).start()

    def relay(t):
        for j in (0, 1, 3, 2):
            for f in (0, 1):
                k_wait(f, t, (3, 1)[t], j)
                k3_copy(f, t, j).start()

    spread(0)
    serve(4)
    spread(1)
    serve(5)
    relay(0)
    serve(6)

    remote(
        qb.at[pl.ds(other * 4, 4)], qb.at[pl.ds(other * 4, 4)], q_s, q_r, dev(x, y, z, other)
    ).wait_recv()
    lane8 = lax.broadcasted_iota(jnp.int32, (8, WIDE), 1)
    pick = jnp.where(
        lane8 == LATENT + ROPE, 64.0, jnp.where(lane8 == LATENT + ROPE + 1, 1.0, 0.0)
    ).astype(BF16)

    def score(f, a):
        posk = dot_nt(pick, kb[f, a].reshape(256, WIDE))[0:1, :]
        for i in range(2):
            bias[:, i * 128 : (i + 1) * 128] = jnp.where(posk[:, i * 128 : (i + 1) * 128] <= posq[...], 0.0, MASKED)
        for p in range(4):
            masks = bias[...]
            scores[f * 4 + a, p] = dot_nt(
                qb[2 * p : 2 * p + 2].reshape(256, WIDE), kb[f, a].reshape(256, WIDE)
            ) + jnp.concatenate([masks, masks], axis=0)

    step = 7
    for i in (0, 1, 3, 2):
        for f in (0, 1):
            if i:
                for t in (0, 1):
                    if (i, t) not in ((3, 0), (1, 1)):
                        for j in range(4):
                            k_wait(f, t, i, j)
            score(f, (place(f)[0] + i) % 4)
            if (i, f) == (0, 0):
                relay(1)
            elif f == 1:
                serve(step)
                step += 1

    def soften(p):
        parts_of = [scores[u, p] for u in range(8)]
        largest = parts_of[0]
        for one in parts_of[1:]:
            largest = jnp.maximum(largest, one)
        largest = jnp.max(largest, axis=1, keepdims=True)
        terms = [jnp.exp2(one - largest) for one in parts_of]
        sums = terms[0]
        for one in terms[1:]:
            sums = sums + one
        sums = jnp.sum(sums, axis=1, keepdims=True)
        mixed = jnp.dot(
            jnp.concatenate([one.astype(BF16) for one in terms], axis=1),
            kb[:, :, :, :, :LATENT].reshape(2048, LATENT),
            preferred_element_type=F32,
        )
        return mixed / sums, jnp.broadcast_to(largest + jnp.log2(sums), (256, 128))

    def m_copy(t, i):
        src, dst = ((o_out, o_in), (lse_out, lse_in))[i]
        return remote(src.at[t], dst.at[t], m_s.at[t, i], m_r.at[t, i], dev(x, y, z, other))

    def a_copy(t, i):
        r = xh if i < 2 else 1 - xh
        to = dev((x + 2) % 4, y, z, core) if i == 0 else dev(x, y, z, other)
        return remote(ab.at[core, t, r], ab.at[core, t, r], a_s.at[t, i], a_r.at[t, core, r], to)

    def a_wait(t, k, r):
        remote(ab.at[k, t, r], ab.at[k, t, r], a_s.at[t, 0], a_r.at[t, k, r], dev(x, y, z, other)).wait_recv()

    for t in range(2):
        mixed, lse_out[t] = soften(other * 2 + t)
        o_out[t] = mixed.astype(BF16)
        for i in range(2):
            m_copy(t, i).start()
    serve(step)
    for t in range(2):
        mixed, lse = soften(core * 2 + t)
        for i in range(2):
            m_copy(t, i).wait_recv()
        largest = jnp.maximum(lse, lse_in[t])
        one, two = jnp.exp2(lse - largest), jnp.exp2(lse_in[t] - largest)
        share = two / (one + two)
        merged = mixed * (one / (one + two))[:, :1] + o_in[t].astype(F32) * share[:, :1]
        merged = merged.astype(BF16)
        for i in range(2):
            n = t * 2 + i
            ab[core, t, xh, :, i * 128 : (i + 1) * 128] = jnp.dot(
                merged[i * 128 : (i + 1) * 128], up_ref[:, 256 * n + 128 : 256 * n + 256], preferred_element_type=F32
            ).astype(BF16)
        a_copy(t, 0).start()
        a_copy(t, 1).start()
    for t in range(2):
        a_wait(t, core, 1 - xh)
        a_copy(t, 2).start()
    for t in range(2):
        a_wait(t, other, xh)
        a_wait(t, other, 1 - xh)

    def p_copy(slot, r):
        dist = (slot + 1) // 2
        zb = (z - dist) % 16 if slot % 2 else (z + dist) % 16
        head = (xh * 16 + zb) // 2
        dst = parts.at[chip, zb % 2, core]
        return (
            jnp.logical_and(head == h, xh == r),
            remote(stage.at[slot, r], dst, p_s.at[slot, r], p_r, (r * 16 + z, head)),
            pltpu.make_async_copy(stage.at[slot, r], dst, p_r),
        )

    def project(first, count):
        made = None
        for e in range(2):
            for t in range(2):
                weights = wb[e, first : first + count, :, t * 256 : (t + 1) * 256].reshape(count * 112, 256)
                term = dot_nt(weights, ab[e, t].reshape(256, 256))
                made = term if made is None else made + term
        made = made.astype(BF16)
        for i in range(count):
            for r in range(2):
                stage[first + i, r] = made[i * 112 : (i + 1) * 112, r * 128 : (r + 1) * 128]
                stays, far, near = p_copy(first + i, r)
                pl.when(jnp.logical_not(stays))(far.start)
                pl.when(stays)(near.start)

    project(0, 4)
    project(4, 5)
    serve(12)
    project(9, 4)
    serve(13)
    project(13, 2)
    serve(14)
    project(15, 1)

    remote(parts, parts, p_s.at[0, 0], p_r, dev(x, y, z, other)).wait_recv()
    result = parts[0].reshape(448, 128).astype(F32)
    for i in range(1, 8):
        result = result + parts[i].reshape(448, 128).astype(F32)
    out_ref[...] = result.astype(BF16)

    @pl.when(mine)
    def _():
        for o in z_order:
            z_copy(o).wait_send()

    for f in (0, 1):
        for t in (0, 1):
            for i in (1, 2, 3):
                k1_copy(f, t, i).wait_send()
            for j in range(4):
                k3_copy(f, t, j).wait_send()
                for side in (0, 1):
                    k2_copy(f, t, j, side).wait_send()
    wx.wait_send()
    q_copy.wait_send()
    for way in (0, 1):
        for u in range(15):
            w_copy(way, u).wait_send()
    for t in range(2):
        for i in range(2):
            m_copy(t, i).wait_send()
        for i in range(3):
            a_copy(t, i).wait_send()

    for slot in range(16):
        for r in range(2):
            stays, far, _ = p_copy(slot, r)
            pl.when(jnp.logical_not(stays))(far.wait_send)


def shards(queries, latents, latent_gain, latent_up, out_weight, positions):
    dma = pltpu.SemaphoreType.DMA
    vmem = pltpu.VMEM
    made = pl.pallas_call(
        kernel,
        out_shape=jax.ShapeDtypeStruct((448, 128), BF16),
        in_specs=[pl.BlockSpec(memory_space=pltpu.HBM)] * 6,
        out_specs=pl.BlockSpec(memory_space=pltpu.VMEM),
        scratch_shapes=[
            vmem((128, 768), BF16),
            vmem((576, 128), BF16),
            vmem((1, 512), F32),
            vmem((512, 1024), BF16),
            vmem((1, 128), jnp.int32),
            vmem((128, WIDE), BF16),
            vmem((2, 4, 4, 64, WIDE), BF16),
            vmem((8, 128, WIDE), BF16),
            vmem((2, 16, 112, 512), BF16),
            vmem((2, 2, 2, 128, 256), BF16),
            vmem((8, 4, 256, 256), F32),
            vmem((128, 128), F32),
            vmem((128, 256), F32),
            vmem((2, 256, 512), BF16),
            vmem((2, 256, 512), BF16),
            vmem((2, 256, 128), F32),
            vmem((2, 256, 128), F32),
            vmem((16, 2, 112, 128), BF16),
            vmem((8, 2, 2, 112, 128), BF16),
            dma((15,)), dma((8,)),
            dma((2, 2, 3)), dma((2, 2, 4, 2)), dma((2, 2, 4)), dma((2, 4, 4, 2)),
            dma, dma, dma, dma,
            dma((2, 15)), dma((2, 15)), dma((2, 2)), dma((2, 2)),
            dma((2, 3)), dma((2, 2, 2)), dma((16, 2)), dma, dma((6,)),
        ],
        compiler_params=pltpu.CompilerParams(
            collective_id=0, has_side_effects=True, vmem_limit_bytes=62 * 1024 * 1024
        ),
        cost_estimate=pl.CostEstimate(flops=8_000_000_000, bytes_accessed=4_000_000, transcendentals=2_200_000),
    )(
        queries, latents.T, latent_gain.reshape(1, 512), latent_up, out_weight.T, positions.reshape(1, 128)
    )
    return made.T


def solution(mesh):
    in_specs = (P("ctx", "head"), P("ctx", None), P(), P(None, "head"), P("head", "ctx"), P("ctx"))
    out_specs = P("ctx", "head")
    return jax.shard_map(shards, mesh=mesh, in_specs=in_specs, out_specs=out_specs, check_vma=False)
```

time: 102 us -> 87 us (0.85); the launches traced: 101 us -> 86.8 us
  Pallas kernels: 95.3 us -> 85.3 us
  local copies, waits for them, and re-layouts: 5.33 us -> 1.55 us
    pallas_call x1, Pallas kernels: 95.3 us -> 85.3 us  [shards(): pl.pallas_call(kernel, out_shape=jax.ShapeDtypeStruct((448, 128), BF16),...]
    unnamed x13 -> x1, local copies, waits for them, and re-layouts: 5.33 us -> 1.55 us
where the time goes in v2:
time: 87 us; the launch traced here: 86.8 us
  Pallas kernels  85.3 us (98%)
  local copies, waits for them, and re-layouts  1.55 us (2%)
    pallas_call x1, Pallas kernels, shards(): pl.pallas_call(kernel, out_shape=jax.ShapeDtypeStruct((448, 128), BF16),...  85.3 us

profile of v2, /device:TPU:7, one launch (start us, length us, event | category | flops | bytes accessed | tf_op | source)
XLA Modules:
  0.0 86.8 jit_solution(791721156325211201)
XLA Ops:
  0.0 85.3 %shard_map.64 = bf16[448,128]{1,0:T(8,128)(2,1)} custom-call(bf16[128,768]{1,0:T(8,128)(2,1)} %q_hbm.1, bf16[576,128]{1,0:T(8,128)(2,1)} %bitcast.7, f32[1,512]{1,0:T(1,128)} %bitcast.8, bf16[512,1024]{1,0:T(8,128)(2,1)} %up_hbm.1, bf16[224,512]{1,0:T(8,128)(2,1)} %bitcast.6, s32[1,128]{1,0:T(1,128)} %bitcast.9), custom_call_target="tpu_custom_call" | custom-call | flops 8000000000 | bytes 4000000 | tf_op jit(solution)/shard_map/pallas_call | solution.py:415
  85.3 1.6 %copy.8 = bf16[128,448]{0,1:T(8,128)(2,1)} copy(bf16[128,448]{0,1:T(8,128)(2,1)} %bitcast.5) | data formatting | bytes 229376

commit v3 on v2

--- a/solution.py
+++ b/solution.py
@@ -28,9 +28,9 @@
     q_hbm, lat_hbm, gain_hbm, up_hbm, wo_hbm, pos_hbm, out_ref,
     q_ref, lat_ref, gain_ref, up_ref, pos_ref,
     own, kb, qb, wb, ab, scores, posq, bias,
-    o_out, o_in, lse_out, lse_in, stage, parts,
-    z_s, z_r, k1_s, k2_s, k3_s, k_r, wx_s, wx_r, q_s, q_r,
-    w_s, w_r, m_s, m_r, a_s, a_r, p_s, p_r, in_s,
+    o_out, o_in, lse_out, lse_in, stage, across, halves, parts,
+    za_s, za_r, zb_s, zb_r, k1_s, k2_s, k3_s, k_r, wx_s, wx_r, q_s, q_r,
+    w_s, w_r, m_s, m_r, a_s, a_r, p_s, p_r, s_s, s_r, in_s,
 ):
     c = lax.axis_index("ctx")
     h = lax.axis_index("head")
@@ -48,18 +48,21 @@
             src_ref=src, dst_ref=dst, send_sem=send, recv_sem=recv, device_id=to, device_id_type=MESH
         )
 
+    def wo_part(k, t):
+        return wo_hbm.at[pl.ds(pl.multiple_of(k * 112, 16), 112), pl.ds(256 * t, 256)]
+
     loads = [
         pltpu.make_async_copy(src, dst, in_s.at[i])
         for i, (src, dst) in enumerate((
             (pos_hbm, pos_ref), (lat_hbm, lat_ref), (gain_hbm, gain_ref), (q_hbm, q_ref), (up_hbm, up_ref),
-            (wo_hbm.at[pl.ds(pl.multiple_of(core * 112, 16), 112)], wb.at[core, 0]),
+            (wo_part(core, 0), wb.at[core, 0, 0]), (wo_part(core, 1), wb.at[core, 1, 0]),
         ))
     ]
     for load in loads:
         load.start()
 
     barrier = pltpu.get_barrier_semaphore()
-    for o in range(1, 16):
+    for o in (1, 15, 2, 14, 4, 12, 8):
         pl.semaphore_signal(barrier, inc=1, device_id=dev(x, y, (z + o) % 16, core), device_id_type=MESH)
     for dx in range(4):
         for dy in range(4):
@@ -69,38 +72,38 @@
                     pl.semaphore_signal(barrier, inc=1, device_id=to, device_id_type=MESH)
 
 
-    wx = remote(
-        wo_hbm.at[pl.ds(pl.multiple_of(other * 112, 16), 112)], wb.at[core, 0], wx_s, wx_r, dev(x, y, z, other)
-    )
-    pl.semaphore_wait(barrier, 46)
-    wx.start()
+    wx = [
+        remote(wo_part(other, t), wb.at[core, t, 0], wx_s.at[t], wx_r.at[t], dev(x, y, z, other)) for t in range(2)
+    ]
+    pl.semaphore_wait(barrier, 38)
+    for copy in wx:
+        copy.start()
 
     def slot_of(way, dist):
         return 0 if dist == 0 else 15 if dist == 8 else 2 * dist - 1 + way
 
     def w_copy(way, u):
-        dist = u // 2 + 1
-        head = core if u % 2 == 0 and not (u == 14 and way == 1) else other
+        dist, t = u // 4 + 1, u % 2
+        head = core if (u % 4 < 2) != (dist == 8 and way == 1) else other
         near = (z + 1) % 16 if way == 0 else (z + 15) % 16
         return remote(
-            wb.at[head, slot_of(way, dist - 1)], wb.at[head, slot_of(way, dist)],
+            wb.at[head, t, slot_of(way, dist - 1)], wb.at[head, t, slot_of(way, dist)],
             w_s.at[way, u], w_r.at[way, u], dev(x, y, near, core),
         )
 
-    def w_wait(way, u):
-        w_copy(way, u).wait_recv()
-
-    def serve(u):
+    def serve(k):
+        for u in (2 * k, 2 * k + 1):
+            for way in (0, 1):
+                w_copy(way, u).wait_recv()
+                if u < 24:
+                    w_copy(way, u + 4).start()
+                elif u < 28 and (u - 24) // 2 == way:
+                    w_copy(way, 28 + u % 2).start()
+
+    for u in (0, 1):
+        loads[5 + u].wait()
         for way in (0, 1):
-            w_wait(way, u)
-            if u < 12:
-                w_copy(way, u + 2).start()
-            elif (u, way) in ((12, 0), (13, 1)):
-                w_copy(way, 14).start()
-
-    loads[5].wait()
-    for way in (0, 1):
-        w_copy(way, 0).start()
+            w_copy(way, u).start()
 
     for load in loads[:3]:
         load.wait()
@@ -128,37 +131,35 @@
 
     mine = (z % 2) == core
     slice_rows = pl.ds(pl.multiple_of(chip * 16, 16), 16)
-    from_even = (0, -2, 2, -4, 4, -6, 6, 8)
-    from_odd = (-1, 1, -3, 3, -5, 5, -7, 7)
 
     def place(f):
         return (y, x) if f == 0 else (x, y)
 
-    def slice_at(n):
-        f, t = (n // 2) % 2, n // 4
-        return kb.at[(f, *place(f), pl.ds(32 * t + 16 * (n % 2), 16))]
-
-    def z_copy(o):
-        n = from_odd.index(-o) if o % 2 else from_even.index(8 if o == 8 else -o)
+    def za_copy(i):
         return remote(
-            own.at[slice_rows], slice_at(n), z_s.at[o % 16 - 1], z_r.at[n], dev(x, y, (z + o) % 16, core)
-        )
-
-    def z_wait(n):
-        remote(slice_at(n), slice_at(n), z_s.at[0], z_r.at[n], dev(x, y, z, other)).wait_recv()
-
-    z_order = (1, -1, 2, -2, 3, -3, 4, -4, 5, -5, 6, -6, 7, -7, 8)
+            own.at[slice_rows], kb.at[0, y, x, pl.ds(16 * i, 16)], za_s.at[i - 1], za_r.at[i - 1],
+            dev(x, y, (z + 4 * i) % 16, core),
+        )
+
+    def zb_copy(i, t):
+        f = min(i, 1)
+        return remote(
+            kb.at[0, y, x, pl.ds(32 * t, 32)], kb.at[(f, *place(f), pl.ds(32 * t, 32))],
+            zb_s.at[i, t], zb_r.at[f, t], dev(x, y, (z + (1, 15, 2)[i]) % 16, core),
+        )
 
     @pl.when(mine)
     def _():
-        for o in z_order:
-            z_copy(o).start()
+        for i in (1, 3, 2):
+            za_copy(i).start()
         kb[0, y, x, 0:16, :] = own[slice_rows, :]
 
-    wx_in = remote(wb.at[other, 0], wb.at[other, 0], wx_s, wx_r, dev(x, y, z, other))
-    wx_in.wait_recv()
-    for way in (0, 1):
-        w_copy(way, 1).start()
+    for u in (2, 3):
+        t = u % 2
+        mine_now = wb.at[other, t, 0]
+        remote(mine_now, mine_now, wx_s.at[t], wx_r.at[t], dev(x, y, z, other)).wait_recv()
+        for way in (0, 1):
+            w_copy(way, u).start()
 
     for load in loads[3:5]:
         load.wait()
@@ -213,18 +214,26 @@
         ref, got = piece(f, (a + i) % 4, (b + j) % 4, t)
         remote(ref, ref, k3_s.at[f, t, 0], got, dev(x, y, z, other)).wait_recv()
 
-    for part in range(4):
-        f, t = part % 2, part // 2
-        if part == 0:
-            pl.when(jnp.logical_not(mine))(functools.partial(z_wait, 0))
+    serve(0)
+    for f, t in ((0, 0), (0, 1), (1, 0), (1, 1)):
+        if f == 0:
+
+            @pl.when(mine)
+            def _():
+                for i in ((1,), (2, 3))[t]:
+                    za_copy(i).wait_recv()
+                for i in range(3):
+                    zb_copy(i, t).start()
+
+            pl.when(jnp.logical_not(mine))(zb_copy(0, t).wait_recv)
         else:
-            z_wait(2 * part)
-        z_wait(2 * part + 1)
+            zb_copy(1, t).wait_recv()
         for i in (1, 3, 2):
             k1_copy(f, t, i).start()
         for side in (0, 1):
             k2_copy(f, t, 0, side).start()
-        serve(part)
+        if t == 1:
+            serve(f + 1)
 
     def spread(t):
         for j in (1, 3, 2):
@@ -240,11 +249,11 @@
                 k3_copy(f, t, j).start()
 
     spread(0)
+    serve(3)
+    spread(1)
     serve(4)
-    spread(1)
+    relay(0)
     serve(5)
-    relay(0)
-    serve(6)
 
     remote(
         qb.at[pl.ds(other * 4, 4)], qb.at[pl.ds(other * 4, 4)], q_s, q_r, dev(x, y, z, other)
@@ -264,7 +273,7 @@
                 qb[2 * p : 2 * p + 2].reshape(256, WIDE), kb[f, a].reshape(256, WIDE)
             ) + jnp.concatenate([masks, masks], axis=0)
 
-    step = 7
+    step = 6
     for i in (0, 1, 3, 2):
         for f in (0, 1):
             if i:
@@ -314,7 +323,7 @@
         o_out[t] = mixed.astype(BF16)
         for i in range(2):
             m_copy(t, i).start()
-    serve(step)
+    serve(10)
     for t in range(2):
         mixed, lse = soften(core * 2 + t)
         for i in range(2):
@@ -331,58 +340,13 @@
             ).astype(BF16)
         a_copy(t, 0).start()
         a_copy(t, 1).start()
-    for t in range(2):
-        a_wait(t, core, 1 - xh)
-        a_copy(t, 2).start()
-    for t in range(2):
-        a_wait(t, other, xh)
-        a_wait(t, other, 1 - xh)
-
-    def p_copy(slot, r):
-        dist = (slot + 1) // 2
-        zb = (z - dist) % 16 if slot % 2 else (z + dist) % 16
-        head = (xh * 16 + zb) // 2
-        dst = parts.at[chip, zb % 2, core]
-        return (
-            jnp.logical_and(head == h, xh == r),
-            remote(stage.at[slot, r], dst, p_s.at[slot, r], p_r, (r * 16 + z, head)),
-            pltpu.make_async_copy(stage.at[slot, r], dst, p_r),
-        )
-
-    def project(first, count):
-        made = None
-        for e in range(2):
-            for t in range(2):
-                weights = wb[e, first : first + count, :, t * 256 : (t + 1) * 256].reshape(count * 112, 256)
-                term = dot_nt(weights, ab[e, t].reshape(256, 256))
-                made = term if made is None else made + term
-        made = made.astype(BF16)
-        for i in range(count):
-            for r in range(2):
-                stage[first + i, r] = made[i * 112 : (i + 1) * 112, r * 128 : (r + 1) * 128]
-                stays, far, near = p_copy(first + i, r)
-                pl.when(jnp.logical_not(stays))(far.start)
-                pl.when(stays)(near.start)
-
-    project(0, 4)
-    project(4, 5)
-    serve(12)
-    project(9, 4)
-    serve(13)
-    project(13, 2)
-    serve(14)
-    project(15, 1)
-
-    remote(parts, parts, p_s.at[0, 0], p_r, dev(x, y, z, other)).wait_recv()
-    result = parts[0].reshape(448, 128).astype(F32)
-    for i in range(1, 8):
-        result = result + parts[i].reshape(448, 128).astype(F32)
-    out_ref[...] = result.astype(BF16)
-
+        serve(11 + t)
     @pl.when(mine)
     def _():
-        for o in z_order:
-            z_copy(o).wait_send()
+        for i in (1, 2, 3):
+            za_copy(i).wait_send()
+            for t in (0, 1):
+                zb_copy(i - 1, t).wait_send()
 
     for f in (0, 1):
         for t in (0, 1):
@@ -392,10 +356,71 @@
                 k3_copy(f, t, j).wait_send()
                 for side in (0, 1):
                     k2_copy(f, t, j, side).wait_send()
-    wx.wait_send()
+
+    for t in range(2):
+        a_wait(t, core, 1 - xh)
+        a_copy(t, 2).start()
+    for t in range(2):
+        a_wait(t, other, xh)
+        a_wait(t, other, 1 - xh)
+
+    def p_copy(slot, r):
+        dist = (slot + 1) // 2
+        zb = (z - dist) % 16 if slot % 2 else (z + dist) % 16
+        to = r * 2 + (zb // 4) % 2
+        dst, got = across.at[zb // 8, x, zb % 4], p_r.at[zb // 8]
+        return (
+            to == x,
+            remote(stage.at[slot, r], dst, p_s.at[slot, r], got, dev(to, y, z, core)),
+            pltpu.make_async_copy(stage.at[slot, r], dst, got),
+        )
+
+    def s_copy(g, j, k):
+        src, dst = halves.at[g, j, pl.ds(2 * k, 2)], parts.at[y, core]
+        return (
+            jnp.logical_and(2 * j + g == y, k == core),
+            remote(src, dst, s_s.at[g, j, k], s_r, dev(x, 2 * j + g, z, k)),
+            pltpu.make_async_copy(src, dst, s_r),
+        )
+
+    def launch(copies):
+        stays, far, near = copies
+        pl.when(jnp.logical_not(stays))(far.start)
+        pl.when(stays)(near.start)
+
+    def fold(g):
+        remote(across.at[g], across.at[g], p_s.at[0, 0], p_r.at[g], dev(x, y, z, other)).wait_recv()
+        for j in range(2):
+            halves[g, j] = (across[g, 2 * j].astype(F32) + across[g, 2 * j + 1].astype(F32)).astype(BF16)
+            for k in range(2):
+                launch(s_copy(g, j, k))
+
+    def project(first, count):
+        made = None
+        for e in range(2):
+            for t in range(2):
+                weights = wb[e, t, first : first + count].reshape(count * 112, 256)
+                term = dot_nt(weights, ab[e, t].reshape(256, 256))
+                made = term if made is None else made + term
+        made = made.astype(BF16)
+        for i in range(count):
+            for r in range(2):
+                stage[first + i, r] = made[i * 112 : (i + 1) * 112, r * 128 : (r + 1) * 128]
+                launch(p_copy(first + i, r))
+
+    project(0, 4)
+    project(4, 5)
+    project(9, 4)
+    serve(13)
+    project(13, 2)
+    serve(14)
+    project(15, 1)
+
+    for copy in wx:
+        copy.wait_send()
     q_copy.wait_send()
     for way in (0, 1):
-        for u in range(15):
+        for u in range(30):
             w_copy(way, u).wait_send()
     for t in range(2):
         for i in range(2):
@@ -403,10 +428,26 @@
         for i in range(3):
             a_copy(t, i).wait_send()
 
+    near_half = z // 8
+    fold(near_half)
+    fold(1 - near_half)
     for slot in range(16):
         for r in range(2):
             stays, far, _ = p_copy(slot, r)
             pl.when(jnp.logical_not(stays))(far.wait_send)
+    remote(parts, parts, s_s.at[0, 0, 0], s_r, dev(x, y, z, other)).wait_recv()
+    for k in range(2):
+        for i in range(2):
+            result = parts[0, k, i].astype(F32)
+            for yy in range(1, 4):
+                result = result + parts[yy, k, i].astype(F32)
+            out_ref[i * 224 + k * 112 : i * 224 + (k + 1) * 112, :] = result.astype(BF16)
+
+    for g in range(2):
+        for j in range(2):
+            for k in range(2):
+                stays, far, _ = s_copy(g, j, k)
+                pl.when(jnp.logical_not(stays))(far.wait_send)
 
 
 def shards(queries, latents, latent_gain, latent_up, out_weight, positions):
@@ -426,7 +467,7 @@
             vmem((128, WIDE), BF16),
             vmem((2, 4, 4, 64, WIDE), BF16),
             vmem((8, 128, WIDE), BF16),
-            vmem((2, 16, 112, 512), BF16),
+            vmem((2, 2, 16, 112, 256), BF16),
             vmem((2, 2, 2, 128, 256), BF16),
             vmem((8, 4, 256, 256), F32),
             vmem((128, 128), F32),
@@ -436,12 +477,14 @@
             vmem((2, 256, 128), F32),
             vmem((2, 256, 128), F32),
             vmem((16, 2, 112, 128), BF16),
-            vmem((8, 2, 2, 112, 128), BF16),
-            dma((15,)), dma((8,)),
+            vmem((2, 4, 4, 112, 128), BF16),
+            vmem((2, 2, 4, 112, 128), BF16),
+            vmem((4, 2, 2, 112, 128), BF16),
+            dma((3,)), dma((3,)), dma((3, 2)), dma((2, 2)),
             dma((2, 2, 3)), dma((2, 2, 4, 2)), dma((2, 2, 4)), dma((2, 4, 4, 2)),
-            dma, dma, dma, dma,
-            dma((2, 15)), dma((2, 15)), dma((2, 2)), dma((2, 2)),
-            dma((2, 3)), dma((2, 2, 2)), dma((16, 2)), dma, dma((6,)),
+            dma((2,)), dma((2,)), dma, dma,
+            dma((2, 30)), dma((2, 30)), dma((2, 2)), dma((2, 2)),
+            dma((2, 3)), dma((2, 2, 2)), dma((16, 2)), dma((2,)), dma((2, 2, 2)), dma, dma((7,)),
         ],
         compiler_params=pltpu.CompilerParams(
             collective_id=0, has_side_effects=True, vmem_limit_bytes=62 * 1024 * 1024

time: 87 us -> 84.8 us (0.975)
  Pallas kernels: 85.3 us -> 83.1 us
    pallas_call x1, Pallas kernels: 85.3 us -> 83.1 us  [shards(): pl.pallas_call(kernel, out_shape=jax.ShapeDtypeStruct((448, 128), BF16),...]
where the time goes in v3:
time: 84.8 us; the launch traced here: 84.6 us
  Pallas kernels  83.1 us (98%)
  local copies, waits for them, and re-layouts  1.55 us (2%)
    pallas_call x1, Pallas kernels, shards(): pl.pallas_call(kernel, out_shape=jax.ShapeDtypeStruct((448, 128), BF16),...  83.1 us

profile of v3, /device:TPU:7, one launch (start us, length us, event | category | flops | bytes accessed | tf_op | source)
XLA Modules:
  0.0 84.6 jit_solution(61775417369576089)
XLA Ops:
  0.0 83.1 %shard_map.64 = bf16[448,128]{1,0:T(8,128)(2,1)} custom-call(bf16[128,768]{1,0:T(8,128)(2,1)} %q_hbm.1, bf16[576,128]{1,0:T(8,128)(2,1)} %bitcast.7, f32[1,512]{1,0:T(1,128)} %bitcast.8, bf16[512,1024]{1,0:T(8,128)(2,1)} %up_hbm.1, bf16[224,512]{1,0:T(8,128)(2,1)} %bitcast.6, s32[1,128]{1,0:T(1,128)} %bitcast.9), custom_call_target="tpu_custom_call" | custom-call | flops 8000000000 | bytes 4000000 | tf_op jit(solution)/shard_map/pallas_call | solution.py:456
  83.1 1.6 %copy.8 = bf16[128,448]{0,1:T(8,128)(2,1)} copy(bf16[128,448]{0,1:T(8,128)(2,1)} %bitcast.5) | data formatting | bytes 229376
